TPU v7x, 256 devices: a whole 4x4x8 slice. The times are simulated.
256 devices in a mesh: face: 2 (over core), tile: 128 (over x, z, y).
Axes of the slice: x: 4, y: 4, z: 8, core: 2. Of those that a mesh axis runs over, the one named last changes fastest.
Arguments:
- fwd_tracers: bfloat16 [2, 90, 4, 32768], P(None, None, None, ('face', 'tile')), may hold values from -6 to 6
- fwd_kappa: bfloat16 [90, 4, 32768], P(None, None, ('face', 'tile')), may hold values from 0.049804688 to 2
- send_order: int32 [2, 128, 128], P('face', 'tile'), may hold values from 0 to 127, each once within a row
- recv_place: int32 [2, 128, 128], P('face', 'tile'), may hold values from 0 to 127, each once within a row
- depth_levels: int32 [512, 256], P('tile', 'face'), may hold values from 0 to 90
- horiz_rate: float32 [90], replicated, may hold values from 0.03 to 0.24
- adj_init: float32 [2, 90, 512, 256], P(None, None, 'tile', 'face'), may hold values from -6 to 6
- misfit: float32 [2, 90, 512, 256], P(None, None, 'tile', 'face'), may hold values from -4 to 4
- ctrl_send: int32 [2, 128, 128], P('face', 'tile'), may hold values from 0 to 127, each once within a row
- ctrl_place: int32 [2, 128, 128], P('face', 'tile'), may hold values from 0 to 127, each once within a row
Outputs:
- sensitivity: float32 [2, 90, 4, 32768], P(None, None, None, ('face', 'tile'))
Inputs may be any that keep to these rules, and one draw needn't show every extreme that they name: `send_order`: each row (last dimension) lists every number of 0 to 127 once. `recv_place`: each row (last dimension) lists every number of 0 to 127 once. `ctrl_send`: each row (last dimension) lists every number of 0 to 127 once. `ctrl_place`: each row (last dimension) lists every number of 0 to 127 once.
All inputs are finite; a program needn't handle non-finite values.
Results may differ from a plain program's by a relative error of at most 0.00095.
Values may be sent and summed in bfloat16 or wider, within the bound.
A program may use at most 64 MiB of HBM per device.

v0:
```python
import functools

import jax
import jax.numpy as jnp
from jax import lax
from jax.experimental import pallas as pl
from jax.experimental.pallas import tpu as pltpu
from jax.sharding import PartitionSpec as P

MESH = pl.DeviceIdType.MESH
F32 = jnp.float32
BF16 = jnp.bfloat16
I32 = jnp.int32

LEV = 90
STEPS = 5
LANES = 128
UNROLL = 10
SIDES = ((0, 1), (1, -1))


def ordered(slot, face0, face1):
    return (face0, face1) if slot % 2 == 0 else (face1, face0)


def stack_faces(slot, face0, face1):
    first, second = ordered(slot, face0, face1)
    return jnp.concatenate([first, second], axis=0)


def in_slot(index_array):
    rows = lax.broadcasted_iota(I32, (LANES, LANES), 0)
    return (rows == index_array).astype(F32)


def column_dot(lhs, rhs):
    return lax.dot_general(lhs, rhs, (((1,), (1,)), ((), ())), preferred_element_type=F32)


def row_dot(lhs, rhs):
    return lax.dot_general(lhs, rhs, (((0,), (1,)), ((), ())), preferred_element_type=F32)


def kernel(
    tiles,
    fwd, kap, send_order, recv_place, depth, rate, adj, mis, ctrl_send, ctrl_place,
    out,
    fwd_v, kap_v, so_v, rp_v, depth_v, adj_v, mis_v, cs_v, cp_v,
    coup_v, stage, send_one, land_one,
    meta, metas, half_adj, half_mis, edge_adj, halo_adj, halo_mis, halo_edge, own_adj, own_mis,
    placed, state, middle, keep, factor, inverse, source,
    final, other, send_two, land_two, stage_two,
    local, meta_sem, one_sem, pass_sem, halo_sem, pair_sem, two_sem,
):
    tile = lax.axis_index("tile")
    face = lax.axis_index("face")
    barrier = pltpu.get_barrier_semaphore()

    def to_tile(shift):
        return lax.rem(tile + (shift + tiles), tiles)

    def greet(step, carry):
        pl.semaphore_signal(
            barrier, inc=1, device_id=(face, lax.rem(tile + step, tiles)), device_id_type=MESH
        )
        return carry

    for shift in (-2, -1, 0, 1, 2):
        pl.semaphore_signal(
            barrier, inc=1, device_id=(1 - face, to_tile(shift)), device_id_type=MESH
        )
    lax.fori_loop(1, tiles, greet, 0)

    moves = [
        pltpu.make_async_copy(src, dst, local.at[i])
        for i, (src, dst) in enumerate((
            (fwd, fwd_v.at[:, pl.ds(0, LEV)]),
            (kap, kap_v.at[pl.ds(0, LEV)]),
            (send_order.at[0], so_v),
            (recv_place.at[0], rp_v),
            (depth, depth_v),
            (adj, adj_v),
            (mis, mis_v),
            (ctrl_send.at[0], cs_v),
            (ctrl_place.at[0], cp_v),
            (adj.at[face], own_adj.at[face]),
            (mis.at[face], own_mis.at[face]),
        ))
    ]
    for move in moves:
        move.start()
    fwd_v[0, LEV] = jnp.zeros((4, LANES), BF16)
    fwd_v[1, LEV] = jnp.zeros((4, LANES), BF16)
    kap_v[LEV] = jnp.zeros((4, LANES), BF16)
    coup_v[pl.ds(4 * LEV, 24)] = jnp.zeros((24, LANES), F32)
    stage[:, 3, :] = jnp.zeros((LANES, LANES), F32)

    for move in moves[:4]:
        move.wait()

    def density(level):
        return 0.8 * fwd_v[1, level].astype(F32) - 0.2 * fwd_v[0, level].astype(F32)

    def couple(block, carry):
        above, kappa_above = carry
        for pair in range(5):
            rows = []
            for half in range(2):
                level = block * 10 + pair * 2 + half + 1
                below = density(level)
                kappa_below = kap_v[level].astype(F32)
                contrast = below - above
                rows.append(
                    0.5 * (kappa_above + kappa_below) * (1.0 + 3.0 * jax.nn.sigmoid(-4.0 * contrast))
                )
                above, kappa_above = below, kappa_below
            coup_v[pl.ds(pl.multiple_of(block * 40 + pair * 8, 8), 8)] = jnp.concatenate(rows, axis=0)
        return above, kappa_above

    lax.fori_loop(0, LEV // 10, couple, (density(0), kap_v[0].astype(F32)))

    pick = in_slot(so_v[...]).T.astype(BF16)
    pieces = column_dot(pick, coup_v[...].astype(BF16))
    for part in range(3):
        stage[:, part, :] = pieces[:, part * LANES : (part + 1) * LANES]
    packed = stage[...].astype(BF16)
    send_one[pl.ds(1, tiles)] = packed
    send_one[0] = packed[tiles - 1]
    send_one[tiles + 1] = packed[0]

    moves[4].wait()
    meta[0] = jnp.concatenate([depth_v[...], depth_v[...]], axis=0)
    meta[1] = jnp.broadcast_to(rp_v[...], (8, LANES))
    metas[4 + face] = meta[...]
    moves[5].wait()
    for tracer in range(2):
        half_adj[tracer] = adj_v[tracer].astype(BF16)
        edge_adj[0, tracer] = adj_v[tracer, :, 3:4, :]
        edge_adj[1, tracer] = adj_v[tracer, :, 0:1, :]
    moves[6].wait()
    for tracer in range(2):
        half_mis[tracer] = mis_v[tracer].astype(BF16)

    pl.semaphore_wait(barrier, tiles + 4)

    def remote(src, dst, send_sem, recv_sem, to_face, to):
        pltpu.make_async_remote_copy(
            src_ref=src, dst_ref=dst, send_sem=send_sem, recv_sem=recv_sem,
            device_id=(to_face, to), device_id_type=MESH,
        ).start()

    for shift in (-1, 1, -2, 2):
        for tracer in range(2):
            remote(
                meta, metas.at[2 * (2 - shift) + face],
                meta_sem.at[0], meta_sem.at[1], tracer, to_tile(shift),
            )
    remote(meta, metas.at[4 + face], meta_sem.at[0], meta_sem.at[1], 1 - face, tile)
    remote(
        adj.at[1 - face], own_adj.at[face], pair_sem.at[0], pair_sem.at[1], 1 - face, tile
    )
    remote(
        mis.at[1 - face], own_mis.at[face], pair_sem.at[2], pair_sem.at[3], 1 - face, tile
    )

    def route_one(step, carry):
        to = lax.rem(tile + step, tiles)
        remote(
            send_one.at[pl.ds(to, 3)], land_one.at[0, tile], one_sem.at[0], one_sem.at[1], face, to
        )
        return carry

    lax.fori_loop(1, tiles, route_one, 0)
    self_one = pltpu.make_async_copy(
        send_one.at[pl.ds(tile, 3)], land_one.at[0, tile], local.at[11]
    )
    self_one.start()
    for side, shift in SIDES:
        for tracer in range(2):
            remote(
                half_adj.at[tracer], halo_adj.at[2 * side + face],
                halo_sem.at[0], halo_sem.at[1], tracer, to_tile(shift),
            )
            remote(
                edge_adj.at[side, tracer], halo_edge.at[2 * side + face],
                halo_sem.at[2], halo_sem.at[3], tracer, to_tile(2 * shift),
            )
    for side, shift in SIDES:
        for tracer in range(2):
            remote(
                half_mis.at[tracer], halo_mis.at[2 * side + face],
                halo_sem.at[4], halo_sem.at[5], tracer, to_tile(shift),
            )

    def arrived(ref, semaphore):
        pltpu.make_async_copy(ref, ref, semaphore).wait()

    row = lax.broadcasted_iota(I32, (8, LANES), 0)
    lane = lax.broadcasted_iota(I32, (8, LANES), 1)
    cell = row % 4
    first_cell, last_cell = cell == 0, cell == 3
    first_lane, last_lane = lane == 0, lane == LANES - 1
    low_lane, low_row = lane < LANES // 2, row < 4
    seam_even = low_lane == low_row
    seam_odd = low_lane != low_row

    def neighbours(slot, west, here, east):
        seam = jnp.where(seam_even if slot % 2 == 0 else seam_odd, pltpu.roll(here, 4, 0), 0.0)
        return (
            pltpu.roll(jnp.where(first_cell, east, here), 7, 0),
            pltpu.roll(jnp.where(last_cell, west, here), 1, 0),
            pltpu.roll(jnp.where(first_lane, seam, here), LANES - 1, 1),
            pltpu.roll(jnp.where(last_lane, seam, here), 1, 1),
        )

    arrived(metas.at[pl.ds(0, 9)], meta_sem.at[1])
    depths = []
    for slot in range(5):
        at = tile + (slot - 2)
        inside = jnp.logical_and(at >= 0, at < tiles).astype(F32)
        first, second = ordered(slot, metas[2 * slot, 0], metas[2 * slot + 1, 0])
        depths.append(jnp.where(low_row, first, second).astype(F32) * inside)
    around = [
        neighbours(slot, depths[slot - 1], depths[slot], depths[slot + 1]) for slot in (1, 2, 3)
    ]

    def wet(level, slot):
        return level.astype(F32) < depths[slot]

    def prepare(block, carry):
        for inner in range(5):
            level = block * 5 + inner
            at = level.astype(F32)
            speed = rate[level]
            for slot in (1, 2, 3):
                count = jnp.zeros((8, LANES), F32)
                for beside in around[slot - 1]:
                    count = count + jnp.where(at < beside, 1.0, 0.0)
                keep[level, slot - 1] = 1.0 - speed * count
        return carry

    lax.fori_loop(0, LEV // 5, prepare, 0)

    moves[9].wait()
    arrived(own_adj.at[0], pair_sem.at[1])
    arrived(halo_adj, halo_sem.at[1])
    arrived(halo_edge, halo_sem.at[3])

    def begin(block, carry):
        for inner in range(5):
            level = block * 5 + inner
            tile_of = {
                1: stack_faces(1, halo_adj[0, level].astype(F32), halo_adj[1, level].astype(F32)),
                2: stack_faces(2, own_adj[0, level], own_adj[1, level]),
                3: stack_faces(3, halo_adj[2, level].astype(F32), halo_adj[3, level].astype(F32)),
                0: jnp.where(low_row, halo_edge[0, level], halo_edge[1, level]),
                4: jnp.where(low_row, halo_edge[2, level], halo_edge[3, level]),
            }
            for slot in range(5):
                state[level, slot] = jnp.where(wet(level, slot), tile_of[slot], 0.0)
        return carry

    lax.fori_loop(0, LEV // 5, begin, 0)

    moves[10].wait()
    arrived(own_mis.at[0], pair_sem.at[3])
    arrived(halo_mis, halo_sem.at[5])

    def drive(block, carry):
        for inner in range(5):
            level = block * 5 + inner
            tile_of = {
                1: stack_faces(1, halo_mis[0, level].astype(F32), halo_mis[1, level].astype(F32)),
                2: stack_faces(2, own_mis[0, level], own_mis[1, level]),
                3: stack_faces(3, halo_mis[2, level].astype(F32), halo_mis[3, level].astype(F32)),
            }
            for slot in (1, 2, 3):
                source[level, slot - 1] = jnp.where(wet(level, slot), tile_of[slot], 0.0)
        return carry

    lax.fori_loop(0, LEV // 5, drive, 0)

    self_one.wait()
    arrived(land_one.at[0, pl.ds(0, tiles - 1)], one_sem.at[1])
    remote(land_one.at[0], land_one.at[1], pass_sem.at[0], pass_sem.at[1], 1 - face, tile)
    for source_of in range(2):
        if source_of == 1:
            arrived(land_one.at[1], pass_sem.at[1])
        which = face if source_of == 0 else 1 - face
        for part in range(3):
            stage[...] = land_one[source_of, :, part].astype(F32)
            held = jnp.concatenate([stage[:, i, :] for i in range(3)], axis=1).astype(BF16)
            place = in_slot(metas[2 * (part + 1) + which, 1][0:1, :]).astype(BF16)
            placed[which, part] = row_dot(held, place)

    one = jnp.ones((8, LANES), F32)

    def eliminate(block, carry):
        carry = [(upper / lower, one) for upper, lower in carry]
        for pair in range(UNROLL // 2):
            base = pl.multiple_of(block * (4 * UNROLL) + pair * 8, 8)
            for slot in (1, 2, 3):
                first, second = ordered(
                    slot, placed[0, slot - 1, pl.ds(base, 8)], placed[1, slot - 1, pl.ds(base, 8)]
                )
                couplings = (
                    jnp.where(low_row, first, pltpu.roll(second, 4, 0)),
                    jnp.where(low_row, pltpu.roll(first, 4, 0), second),
                )
                upper, lower = carry[slot - 1]
                for half in range(2):
                    level = block * UNROLL + pair * 2 + half
                    weight = jnp.where(
                        (level + 1).astype(F32) < depths[slot], couplings[half], 0.0
                    )
                    next_lower = upper + weight * lower
                    next_upper = next_lower + weight * upper
                    ratio = lower / next_lower
                    factor[level, slot - 1] = weight * ratio
                    inverse[level, slot - 1] = jnp.where(wet(level, slot), ratio, 0.0)
                    upper, lower = next_upper, next_lower
                carry[slot - 1] = (upper, lower)
        return carry

    lax.fori_loop(0, LEV // UNROLL, eliminate, [(one, one)] * 3)

    zero = jnp.zeros((8, LANES), F32)

    def descend(slots, block, carry):
        carry = list(carry)
        for inner in range(UNROLL):
            level = block * UNROLL + inner
            speed = rate[level]
            tile_of = {
                slot: state[level, slot] for slot in range(slots[0] - 1, slots[-1] + 2)
            }
            for i, slot in enumerate(slots):
                east, west, north, south = neighbours(
                    slot, tile_of[slot - 1], tile_of[slot], tile_of[slot + 1]
                )
                spread = keep[level, slot - 1] * tile_of[slot] + speed * (
                    (east + west) + (north + south)
                )
                value = spread + carry[i]
                middle[level, slot - 1] = value
                carry[i] = factor[level, slot - 1] * value
        return carry

    def ascend(slots, last, block, carry):
        carry = list(carry)
        for pair in range(UNROLL // 2):
            halves = []
            for inner in range(2):
                level = (LEV - 1) - (block * UNROLL + pair * 2 + inner)
                for i, slot in enumerate(slots):
                    solved = (
                        middle[level, slot - 1] * inverse[level, slot - 1]
                        + factor[level, slot - 1] * carry[i]
                    )
                    carry[i] = solved
                    value = solved + source[level, slot - 1]
                    if last:
                        halves.append(value)
                    else:
                        state[level, slot] = value
            if last:
                below, above = halves
                base = pl.multiple_of(
                    (4 * LEV - 8) - (block * (4 * UNROLL) + pair * 8), 8
                )
                final[0, pl.ds(base, 8)] = jnp.where(low_row, above, pltpu.roll(below, 4, 0))
                final[1, pl.ds(base, 8)] = jnp.where(low_row, pltpu.roll(above, 4, 0), below)
        return carry

    def advance(step, carry):
        lax.fori_loop(0, LEV // UNROLL, functools.partial(descend, (1, 2, 3)), [zero] * 3)
        lax.fori_loop(0, LEV // UNROLL, functools.partial(ascend, (1, 2, 3), False), [zero] * 3)
        return carry

    lax.fori_loop(0, STEPS - 1, advance, 0)
    lax.fori_loop(0, LEV // UNROLL, functools.partial(descend, (2,)), [zero])
    final[0, pl.ds(4 * LEV, 24)] = jnp.zeros((24, LANES), F32)
    final[1, pl.ds(4 * LEV, 24)] = jnp.zeros((24, LANES), F32)
    lax.fori_loop(0, LEV // UNROLL, functools.partial(ascend, (2,), True), [zero])

    remote(final.at[1 - face], other, pair_sem.at[4], pair_sem.at[5], 1 - face, tile)
    moves[7].wait()
    moves[8].wait()
    choose = in_slot(cs_v[...]).T.astype(BF16)
    for source_of in range(2):
        if source_of == 0:
            values, tracer = final[face], face
        else:
            arrived(other, pair_sem.at[5])
            values, tracer = other[...], 1 - face
        high = values.astype(BF16)
        low = (values - high.astype(F32)).astype(BF16)
        pieces = column_dot(choose, high) + column_dot(choose, low)
        for part in range(3):
            stage_two[tracer, :, part, :] = pieces[:, part * LANES : (part + 1) * LANES]
    for part in range(6):
        send_two[:, part // 2, part % 2, :] = stage_two[part // 3, :, part % 3, :]

    def route_two(step, carry):
        to = lax.rem(tile + step, tiles)
        remote(send_two.at[to], land_two.at[tile], two_sem.at[0], two_sem.at[1], face, to)
        return carry

    lax.fori_loop(1, tiles, route_two, 0)
    self_two = pltpu.make_async_copy(send_two.at[tile], land_two.at[tile], local.at[12])
    self_two.start()
    place = in_slot(cp_v[...]).astype(BF16)
    self_two.wait()
    arrived(land_two.at[pl.ds(0, tiles - 1)], two_sem.at[1])
    for tracer in range(2):
        values = jnp.concatenate(
            [land_two[:, part // 2, part % 2, :] for part in range(3 * tracer, 3 * tracer + 3)],
            axis=1,
        )
        high = values.astype(BF16)
        low = (values - high.astype(F32)).astype(BF16)
        result = row_dot(high, place) + row_dot(low, place)
        out[tracer] = result[: 4 * LEV].reshape(LEV, 4, LANES)

    arrived(metas.at[pl.ds(0, 9)], meta_sem.at[0])
    arrived(own_adj.at[0], pair_sem.at[0])
    arrived(own_mis.at[0], pair_sem.at[2])
    arrived(land_one.at[0, pl.ds(0, tiles - 1)], one_sem.at[0])
    arrived(halo_adj, halo_sem.at[0])
    arrived(halo_edge, halo_sem.at[2])
    arrived(halo_mis, halo_sem.at[4])
    arrived(land_one.at[1], pass_sem.at[0])
    arrived(other, pair_sem.at[4])
    arrived(land_two.at[pl.ds(0, tiles - 1)], two_sem.at[0])


def per_device(
    fwd_tracers, fwd_kappa, send_order, recv_place, depth_levels, horiz_rate, adj_init, misfit,
    ctrl_send, ctrl_place,
):
    tiles = lax.axis_size("tile")
    anywhere = pl.BlockSpec(memory_space=pl.ANY)
    vmem = pltpu.VMEM
    dma = pltpu.SemaphoreType.DMA
    block = (LEV, 4, LANES)
    level_rows = (LEV, 3, 8, LANES)
    scratch = [
        vmem((2, LEV + 1, 4, LANES), BF16), vmem((LEV + 1, 4, LANES), BF16),
        vmem((1, LANES), I32), vmem((1, LANES), I32), vmem((4, LANES), I32),
        vmem((2,) + block, F32), vmem((2,) + block, F32),
        vmem((1, LANES), I32), vmem((1, LANES), I32),
        vmem((384, LANES), F32), vmem((tiles, 4, LANES), F32),
        vmem((tiles + 2, 4, LANES), BF16), vmem((2, tiles, 3, 4, LANES), BF16),
        vmem((2, 8, LANES), I32), vmem((10, 2, 8, LANES), I32),
        vmem((2,) + block, BF16), vmem((2,) + block, BF16), vmem((2, 2, LEV, 1, LANES), F32),
        vmem((4,) + block, BF16), vmem((4,) + block, BF16), vmem((4, LEV, 1, LANES), F32),
        vmem((2,) + block, F32), vmem((2,) + block, F32),
        vmem((2, 3, 384, LANES), F32), vmem((LEV, 5, 8, LANES), F32),
        vmem(level_rows, F32), vmem(level_rows, F32), vmem(level_rows, F32),
        vmem(level_rows, F32), vmem(level_rows, F32),
        vmem((2, 384, LANES), F32), vmem((384, LANES), F32),
        vmem((tiles, 3, 2, LANES), F32), vmem((tiles, 3, 2, LANES), F32),
        vmem((2, tiles, 3, LANES), F32),
        dma((13,)), dma((2,)), dma((2,)), dma((2,)), dma((6,)), dma((6,)), dma((2,)),
    ]
    return pl.pallas_call(
        functools.partial(kernel, tiles),
        out_shape=jax.ShapeDtypeStruct((2,) + block, F32),
        in_specs=[anywhere] * 5 + [pl.BlockSpec(memory_space=pltpu.SMEM)] + [anywhere] * 4,
        out_specs=pl.BlockSpec(memory_space=pltpu.VMEM),
        scratch_shapes=scratch,
        compiler_params=pltpu.CompilerParams(
            collective_id=0, has_side_effects=True, vmem_limit_bytes=48 * 2**20
        ),
        cost_estimate=pl.CostEstimate(
            flops=10**9, bytes_accessed=4 * 2**20, transcendentals=10**5
        ),
    )(
        fwd_tracers, fwd_kappa, send_order, recv_place, depth_levels, horiz_rate, adj_init, misfit,
        ctrl_send, ctrl_place,
    )


def solution(mesh):
    placed = (
        P(None, None, None, ("face", "tile")),
        P(None, None, ("face", "tile")),
        P("face", "tile", None),
        P("face", "tile", None),
        P("tile", "face"),
        P(),
        P(None, None, "tile", "face"),
        P(None, None, "tile", "face"),
        P("face", "tile", None),
        P("face", "tile", None),
    )
    return jax.shard_map(
        per_device,
        mesh=mesh,
        in_specs=placed,
        out_specs=P(None, None, None, ("face", "tile")),
        check_vma=False,
    )
```

profile of v0, /device:TPU:1, one launch (start us, length us, event | category | flops | bytes accessed | tf_op | source)
XLA Modules:
  0.0 69.4 jit_solution(15584036204580049294)
XLA Ops:
  0.0 0.0 copy-start
  0.0 1.0 %copy-done = f32[2,90,4,128]{3,2,1,0:T(4,128)S(1)} copy-done((f32[2,90,4,128]{3,2,1,0:T(4,128)S(1)}, f32[2,90,4,128]{3,2,1,0:T(4,128)}, u32[]{:S(2)}) %copy-start) | copy-done | bytes 368664
  1.0 0.0 copy-start.1
  1.0 1.0 %copy-done.1 = f32[2,90,4,128]{3,2,1,0:T(4,128)S(1)} copy-done((f32[2,90,4,128]{3,2,1,0:T(4,128)S(1)}, f32[2,90,4,128]{3,2,1,0:T(4,128)}, u32[]{:S(2)}) %copy-start.1) | copy-done | bytes 368664
  2.0 0.0 copy-start.2
  2.0 0.9 %copy-done.2 = bf16[2,90,4,128]{3,2,1,0:T(4,128)(2,1)S(1)} copy-done((bf16[2,90,4,128]{3,2,1,0:T(4,128)(2,1)S(1)}, bf16[2,90,4,128]{3,2,1,0:T(4,128)(2,1)}, u32[]{:S(2)}) %copy-start.2) | copy-done | bytes 184344
  2.9 0.0 copy-start.3
  2.9 0.9 %copy-done.3 = bf16[90,4,128]{2,1,0:T(4,128)(2,1)S(1)} copy-done((bf16[90,4,128]{2,1,0:T(4,128)(2,1)S(1)}, bf16[90,4,128]{2,1,0:T(4,128)(2,1)}, u32[]{:S(2)}) %copy-start.3) | copy-done | bytes 92184
  3.8 0.0 copy-start.4
  3.8 0.7 copy-done.4
  4.5 0.0 copy-start.5
  4.5 0.7 copy-done.5
  5.1 0.0 copy-start.6
  5.1 0.7 copy-done.6
  5.8 0.0 copy-start.7
  5.8 0.7 copy-done.7
  6.4 0.0 copy-start.8
  6.4 0.7 copy-done.8
  7.1 0.0 copy-start.9
  7.1 0.7 copy-done.9
  7.8 60.9 %shard_map.100 = f32[2,90,4,128]{3,2,1,0:T(4,128)S(1)} custom-call(bf16[2,90,4,128]{3,2,1,0:T(4,128)(2,1)S(1)} %copy-done.2, bf16[90,4,128]{2,1,0:T(4,128)(2,1)S(1)} %copy-done.3, s32[1,1,128]{2,1,0:T(1,128)S(1)} %copy-done.5, s32[1,1,128]{2,1,0:T(1,128)S(1)} %copy-done.6, s32[4,128]{1,0:T(4,128)S(1)} %copy-done.4, f32[90]{0:T(128)S(1)} %copy-done.7, ...), custom_call_target="tpu_custom_call" | custom-call | flops 1000000000 | bytes 4194304 | tf_op jit(solution)/shard_map/pallas_call | solution.py:466
  68.7 0.7 %copy.12 = f32[2,90,4,128]{3,2,1,0:T(4,128)} copy(f32[2,90,4,128]{3,2,1,0:T(4,128)S(1)} %shard_map.100) | data formatting | bytes 737280
Async XLA Ops:
  0.0 1.0 %copy-start = (f32[2,90,4,128]{3,2,1,0:T(4,128)S(1)}, f32[2,90,4,128]{3,2,1,0:T(4,128)}, u32[]{:S(2)}) copy-start(f32[2,90,4,128]{3,2,1,0:T(4,128)} %adj.1) | copy-start | bytes 1105924
  1.0 1.0 %copy-start.1 = (f32[2,90,4,128]{3,2,1,0:T(4,128)S(1)}, f32[2,90,4,128]{3,2,1,0:T(4,128)}, u32[]{:S(2)}) copy-start(f32[2,90,4,128]{3,2,1,0:T(4,128)} %mis.1) | copy-start | bytes 1105924
  2.0 0.9 %copy-start.2 = (bf16[2,90,4,128]{3,2,1,0:T(4,128)(2,1)S(1)}, bf16[2,90,4,128]{3,2,1,0:T(4,128)(2,1)}, u32[]{:S(2)}) copy-start(bf16[2,90,4,128]{3,2,1,0:T(4,128)(2,1)} %fwd.1) | copy-start | bytes 552964
  2.9 0.9 %copy-start.3 = (bf16[90,4,128]{2,1,0:T(4,128)(2,1)S(1)}, bf16[90,4,128]{2,1,0:T(4,128)(2,1)}, u32[]{:S(2)}) copy-start(bf16[90,4,128]{2,1,0:T(4,128)(2,1)} %kap.1) | copy-start | bytes 276484
  3.8 0.7 copy-start.4
  4.5 0.7 copy-start.5
  5.1 0.7 copy-start.6
  5.8 0.7 copy-start.7
  6.4 0.7 copy-start.8
  7.1 0.7 copy-start.9
where the time goes:
time: 69.7 us; the launch traced here: 69.4 us
  Pallas kernels  60.9 us (87%)
  local copies, waits for them, and re-layouts  8.48 us (12%)
    pallas_call x1, Pallas kernels, per_device(): pl.pallas_call(functools.partial(kernel, tiles), out_shape=jax.ShapeDtype...  60.9 us
    unnamed x21, local copies, waits for them, and re-layouts  8.48 us

commit v1 on v0

--- a/solution.py
+++ b/solution.py
@@ -43,9 +43,9 @@
 
 def kernel(
     tiles,
-    fwd, kap, send_order, recv_place, depth, rate, adj, mis, ctrl_send, ctrl_place,
+    fwd, kap, send_order, recv_place, depth, rate_in, adj, mis, ctrl_send, ctrl_place,
     out,
-    fwd_v, kap_v, so_v, rp_v, depth_v, adj_v, mis_v, cs_v, cp_v,
+    rate, fwd_v, kap_v, so_v, rp_v, depth_v, adj_v, mis_v, cs_v, cp_v,
     coup_v, stage, send_one, land_one,
     meta, metas, half_adj, half_mis, edge_adj, halo_adj, halo_mis, halo_edge, own_adj, own_mis,
     placed, state, middle, keep, factor, inverse, source,
@@ -85,6 +85,7 @@
             (ctrl_place.at[0], cp_v),
             (adj.at[face], own_adj.at[face]),
             (mis.at[face], own_mis.at[face]),
+            (rate_in, rate),
         ))
     ]
     for move in moves:
@@ -172,7 +173,7 @@
 
     lax.fori_loop(1, tiles, route_one, 0)
     self_one = pltpu.make_async_copy(
-        send_one.at[pl.ds(tile, 3)], land_one.at[0, tile], local.at[11]
+        send_one.at[pl.ds(tile, 3)], land_one.at[0, tile], local.at[12]
     )
     self_one.start()
     for side, shift in SIDES:
@@ -239,6 +240,7 @@
                 keep[level, slot - 1] = 1.0 - speed * count
         return carry
 
+    moves[11].wait()
     lax.fori_loop(0, LEV // 5, prepare, 0)
 
     moves[9].wait()
@@ -407,7 +409,7 @@
         return carry
 
     lax.fori_loop(1, tiles, route_two, 0)
-    self_two = pltpu.make_async_copy(send_two.at[tile], land_two.at[tile], local.at[12])
+    self_two = pltpu.make_async_copy(send_two.at[tile], land_two.at[tile], local.at[13])
     self_two.start()
     place = in_slot(cp_v[...]).astype(BF16)
     self_two.wait()
@@ -439,12 +441,13 @@
     ctrl_send, ctrl_place,
 ):
     tiles = lax.axis_size("tile")
-    anywhere = pl.BlockSpec(memory_space=pl.ANY)
+    anywhere = pl.BlockSpec(memory_space=pltpu.HBM)
     vmem = pltpu.VMEM
     dma = pltpu.SemaphoreType.DMA
     block = (LEV, 4, LANES)
     level_rows = (LEV, 3, 8, LANES)
     scratch = [
+        pltpu.SMEM((LEV,), F32),
         vmem((2, LEV + 1, 4, LANES), BF16), vmem((LEV + 1, 4, LANES), BF16),
         vmem((1, LANES), I32), vmem((1, LANES), I32), vmem((4, LANES), I32),
         vmem((2,) + block, F32), vmem((2,) + block, F32),
@@ -461,16 +464,16 @@
         vmem((2, 384, LANES), F32), vmem((384, LANES), F32),
         vmem((tiles, 3, 2, LANES), F32), vmem((tiles, 3, 2, LANES), F32),
         vmem((2, tiles, 3, LANES), F32),
-        dma((13,)), dma((2,)), dma((2,)), dma((2,)), dma((6,)), dma((6,)), dma((2,)),
+        dma((14,)), dma((2,)), dma((2,)), dma((2,)), dma((6,)), dma((6,)), dma((2,)),
     ]
     return pl.pallas_call(
         functools.partial(kernel, tiles),
         out_shape=jax.ShapeDtypeStruct((2,) + block, F32),
-        in_specs=[anywhere] * 5 + [pl.BlockSpec(memory_space=pltpu.SMEM)] + [anywhere] * 4,
+        in_specs=[anywhere] * 10,
         out_specs=pl.BlockSpec(memory_space=pltpu.VMEM),
         scratch_shapes=scratch,
         compiler_params=pltpu.CompilerParams(
-            collective_id=0, has_side_effects=True, vmem_limit_bytes=48 * 2**20
+            collective_id=0, has_side_effects=True, vmem_limit_bytes=60 * 2**20
         ),
         cost_estimate=pl.CostEstimate(
             flops=10**9, bytes_accessed=4 * 2**20, transcendentals=10**5

time: 69.7 us -> 62.9 us (0.902)
  local copies, waits for them, and re-layouts: 8.48 us -> 1.75 us
    unnamed x21 -> x1, local copies, waits for them, and re-layouts: 8.48 us -> 1.75 us
where the time goes in v1:
time: 62.9 us; the launch traced here: 62.7 us
  Pallas kernels  61 us (97%)
  local copies, waits for them, and re-layouts  1.75 us (3%)
    pallas_call x1, Pallas kernels, per_device(): pl.pallas_call(functools.partial(kernel, tiles), out_shape=jax.ShapeDtype...  61 us
    unnamed x1, local copies, waits for them, and re-layouts  1.75 us

profile of v1, /device:TPU:1, one launch (start us, length us, event | category | flops | bytes accessed | tf_op | source)
XLA Modules:
  0.0 62.7 jit_solution(3163316072882460553)
XLA Ops:
  0.0 61.0 %shard_map.100 = f32[2,90,4,128]{3,2,1,0:T(4,128)} custom-call(bf16[2,90,4,128]{3,2,1,0:T(4,128)(2,1)} %fwd.1, bf16[90,4,128]{2,1,0:T(4,128)(2,1)} %kap.1, s32[1,1,128]{2,1,0:T(1,128)} %send_order.1, s32[1,1,128]{2,1,0:T(1,128)} %recv_place.1, s32[4,128]{1,0:T(4,128)} %depth.1, f32[90]{0:T(128)} %rate_in.1, f32[2,90,4,128]{3,2,1,0:T(4,128)} %adj.1, ...), custom_call_target="tpu_custom_call" | custom-call | flops 1000000000 | bytes 4194304 | tf_op jit(solution)/shard_map/pallas_call | solution.py:469
  61.0 1.7 %copy.12 = f32[2,90,4,128]{3,2,1,0:T(4,128)} copy(f32[2,90,4,128]{3,2,1,0:T(4,128)} %shard_map.100) | data formatting | bytes 737280

commit v2 on v1

--- a/solution.py
+++ b/solution.py
@@ -11,11 +11,14 @@
 F32 = jnp.float32
 BF16 = jnp.bfloat16
 I32 = jnp.int32
+I16 = jnp.int16
 
 LEV = 90
 STEPS = 5
 LANES = 128
 UNROLL = 10
+SWEEP = 90
+CODE = 32000.0
 SIDES = ((0, 1), (1, -1))
 
 
@@ -49,7 +52,7 @@
     coup_v, stage, send_one, land_one,
     meta, metas, half_adj, half_mis, edge_adj, halo_adj, halo_mis, halo_edge, own_adj, own_mis,
     placed, state, middle, keep, factor, inverse, source,
-    final, other, send_two, land_two, stage_two,
+    final, other, send_two, land_two, stage_pair, stage_two,
     local, meta_sem, one_sem, pass_sem, halo_sem, pair_sem, two_sem,
 ):
     tile = lax.axis_index("tile")
@@ -243,50 +246,31 @@
     moves[11].wait()
     lax.fori_loop(0, LEV // 5, prepare, 0)
 
-    moves[9].wait()
-    arrived(own_adj.at[0], pair_sem.at[1])
-    arrived(halo_adj, halo_sem.at[1])
-    arrived(halo_edge, halo_sem.at[3])
-
-    def begin(block, carry):
-        for inner in range(5):
-            level = block * 5 + inner
-            tile_of = {
-                1: stack_faces(1, halo_adj[0, level].astype(F32), halo_adj[1, level].astype(F32)),
-                2: stack_faces(2, own_adj[0, level], own_adj[1, level]),
-                3: stack_faces(3, halo_adj[2, level].astype(F32), halo_adj[3, level].astype(F32)),
-                0: jnp.where(low_row, halo_edge[0, level], halo_edge[1, level]),
-                4: jnp.where(low_row, halo_edge[2, level], halo_edge[3, level]),
-            }
-            for slot in range(5):
-                state[level, slot] = jnp.where(wet(level, slot), tile_of[slot], 0.0)
-        return carry
-
-    lax.fori_loop(0, LEV // 5, begin, 0)
-
-    moves[10].wait()
-    arrived(own_mis.at[0], pair_sem.at[3])
-    arrived(halo_mis, halo_sem.at[5])
-
-    def drive(block, carry):
-        for inner in range(5):
-            level = block * 5 + inner
-            tile_of = {
-                1: stack_faces(1, halo_mis[0, level].astype(F32), halo_mis[1, level].astype(F32)),
-                2: stack_faces(2, own_mis[0, level], own_mis[1, level]),
-                3: stack_faces(3, halo_mis[2, level].astype(F32), halo_mis[3, level].astype(F32)),
-            }
-            for slot in (1, 2, 3):
-                source[level, slot - 1] = jnp.where(wet(level, slot), tile_of[slot], 0.0)
-        return carry
-
-    lax.fori_loop(0, LEV // 5, drive, 0)
-
     self_one.wait()
     arrived(land_one.at[0, pl.ds(0, tiles - 1)], one_sem.at[1])
     remote(land_one.at[0], land_one.at[1], pass_sem.at[0], pass_sem.at[1], 1 - face, tile)
     for source_of in range(2):
         if source_of == 1:
+            moves[9].wait()
+            arrived(own_adj.at[0], pair_sem.at[1])
+            arrived(halo_adj, halo_sem.at[1])
+            arrived(halo_edge, halo_sem.at[3])
+
+            def begin(block, carry):
+                for inner in range(5):
+                    level = block * 5 + inner
+                    tile_of = {
+                        1: stack_faces(1, halo_adj[0, level].astype(F32), halo_adj[1, level].astype(F32)),
+                        2: stack_faces(2, own_adj[0, level], own_adj[1, level]),
+                        3: stack_faces(3, halo_adj[2, level].astype(F32), halo_adj[3, level].astype(F32)),
+                        0: jnp.where(low_row, halo_edge[0, level], halo_edge[1, level]),
+                        4: jnp.where(low_row, halo_edge[2, level], halo_edge[3, level]),
+                    }
+                    for slot in range(5):
+                        state[level, slot] = jnp.where(wet(level, slot), tile_of[slot], 0.0)
+                return carry
+
+            lax.fori_loop(0, LEV // 5, begin, 0)
             arrived(land_one.at[1], pass_sem.at[1])
         which = face if source_of == 0 else 1 - face
         for part in range(3):
@@ -330,8 +314,8 @@
 
     def descend(slots, block, carry):
         carry = list(carry)
-        for inner in range(UNROLL):
-            level = block * UNROLL + inner
+        for inner in range(SWEEP):
+            level = block * SWEEP + inner
             speed = rate[level]
             tile_of = {
                 slot: state[level, slot] for slot in range(slots[0] - 1, slots[-1] + 2)
@@ -350,10 +334,10 @@
 
     def ascend(slots, last, block, carry):
         carry = list(carry)
-        for pair in range(UNROLL // 2):
+        for pair in range(SWEEP // 2):
             halves = []
             for inner in range(2):
-                level = (LEV - 1) - (block * UNROLL + pair * 2 + inner)
+                level = (LEV - 1) - (block * SWEEP + pair * 2 + inner)
                 for i, slot in enumerate(slots):
                     solved = (
                         middle[level, slot - 1] * inverse[level, slot - 1]
@@ -368,27 +352,49 @@
             if last:
                 below, above = halves
                 base = pl.multiple_of(
-                    (4 * LEV - 8) - (block * (4 * UNROLL) + pair * 8), 8
+                    (4 * LEV - 8) - (block * (4 * SWEEP) + pair * 8), 8
                 )
                 final[0, pl.ds(base, 8)] = jnp.where(low_row, above, pltpu.roll(below, 4, 0))
                 final[1, pl.ds(base, 8)] = jnp.where(low_row, pltpu.roll(above, 4, 0), below)
         return carry
 
     def advance(step, carry):
-        lax.fori_loop(0, LEV // UNROLL, functools.partial(descend, (1, 2, 3)), [zero] * 3)
-        lax.fori_loop(0, LEV // UNROLL, functools.partial(ascend, (1, 2, 3), False), [zero] * 3)
-        return carry
-
-    lax.fori_loop(0, STEPS - 1, advance, 0)
-    lax.fori_loop(0, LEV // UNROLL, functools.partial(descend, (2,)), [zero])
+        lax.fori_loop(0, LEV // SWEEP, functools.partial(descend, (1, 2, 3)), [zero] * 3)
+        lax.fori_loop(0, LEV // SWEEP, functools.partial(ascend, (1, 2, 3), False), [zero] * 3)
+        return carry
+
+    sweep_down = functools.partial(descend, (1, 2, 3))
+    lax.fori_loop(0, LEV // SWEEP, sweep_down, [zero] * 3)
+    moves[10].wait()
+    arrived(own_mis.at[0], pair_sem.at[3])
+    arrived(halo_mis, halo_sem.at[5])
+
+    def drive(block, carry):
+        for inner in range(5):
+            level = block * 5 + inner
+            tile_of = {
+                1: stack_faces(1, halo_mis[0, level].astype(F32), halo_mis[1, level].astype(F32)),
+                2: stack_faces(2, own_mis[0, level], own_mis[1, level]),
+                3: stack_faces(3, halo_mis[2, level].astype(F32), halo_mis[3, level].astype(F32)),
+            }
+            for slot in (1, 2, 3):
+                source[level, slot - 1] = jnp.where(wet(level, slot), tile_of[slot], 0.0)
+        return carry
+
+    lax.fori_loop(0, LEV // 5, drive, 0)
+
+    lax.fori_loop(0, LEV // SWEEP, functools.partial(ascend, (1, 2, 3), False), [zero] * 3)
+    lax.fori_loop(1, STEPS - 1, advance, 0)
+    lax.fori_loop(0, LEV // SWEEP, functools.partial(descend, (2,)), [zero])
     final[0, pl.ds(4 * LEV, 24)] = jnp.zeros((24, LANES), F32)
     final[1, pl.ds(4 * LEV, 24)] = jnp.zeros((24, LANES), F32)
-    lax.fori_loop(0, LEV // UNROLL, functools.partial(ascend, (2,), True), [zero])
+    lax.fori_loop(0, LEV // SWEEP, functools.partial(ascend, (2,), True), [zero])
 
     remote(final.at[1 - face], other, pair_sem.at[4], pair_sem.at[5], 1 - face, tile)
     moves[7].wait()
     moves[8].wait()
     choose = in_slot(cs_v[...]).T.astype(BF16)
+    end_lane = lax.broadcasted_iota(I32, (LANES, LANES), 1) == LANES - 1
     for source_of in range(2):
         if source_of == 0:
             values, tracer = final[face], face
@@ -398,10 +404,17 @@
         high = values.astype(BF16)
         low = (values - high.astype(F32)).astype(BF16)
         pieces = column_dot(choose, high) + column_dot(choose, low)
+        largest = jnp.max(jnp.abs(pieces), axis=1, keepdims=True)
+        octave = jnp.ceil(4.0 * jnp.log2(jnp.maximum(largest, 1e-33)) + 0.01)
+        codes = jnp.floor(pieces * (CODE / jnp.exp2(0.25 * octave)) + 0.5)
         for part in range(3):
-            stage_two[tracer, :, part, :] = pieces[:, part * LANES : (part + 1) * LANES]
+            column = codes[:, part * LANES : (part + 1) * LANES]
+            if part == 2:
+                column = jnp.where(end_lane, octave, column)
+            stage_two[tracer, :, part, :] = column
     for part in range(6):
-        send_two[:, part // 2, part % 2, :] = stage_two[part // 3, :, part % 3, :]
+        stage_pair[:, part // 2, part % 2, :] = stage_two[part // 3, :, part % 3, :]
+    send_two[...] = stage_pair[...].astype(I32).astype(I16)
 
     def route_two(step, carry):
         to = lax.rem(tile + step, tiles)
@@ -414,11 +427,14 @@
     place = in_slot(cp_v[...]).astype(BF16)
     self_two.wait()
     arrived(land_two.at[pl.ds(0, tiles - 1)], two_sem.at[1])
+    stage_pair[...] = land_two[...].astype(I32).astype(F32)
     for tracer in range(2):
         values = jnp.concatenate(
-            [land_two[:, part // 2, part % 2, :] for part in range(3 * tracer, 3 * tracer + 3)],
+            [stage_pair[:, part // 2, part % 2, :] for part in range(3 * tracer, 3 * tracer + 3)],
             axis=1,
         )
+        octave = values[:, 3 * LANES - 1 :]
+        values = values * (jnp.exp2(0.25 * octave) * (1.0 / CODE))
         high = values.astype(BF16)
         low = (values - high.astype(F32)).astype(BF16)
         result = row_dot(high, place) + row_dot(low, place)
@@ -462,7 +478,8 @@
         vmem(level_rows, F32), vmem(level_rows, F32), vmem(level_rows, F32),
         vmem(level_rows, F32), vmem(level_rows, F32),
         vmem((2, 384, LANES), F32), vmem((384, LANES), F32),
-        vmem((tiles, 3, 2, LANES), F32), vmem((tiles, 3, 2, LANES), F32),
+        vmem((tiles, 3, 2, LANES), I16), vmem((tiles, 3, 2, LANES), I16),
+        vmem((tiles, 3, 2, LANES), F32),
         vmem((2, tiles, 3, LANES), F32),
         dma((14,)), dma((2,)), dma((2,)), dma((2,)), dma((6,)), dma((6,)), dma((2,)),
     ]

time: 62.9 us -> 51.4 us (0.82)
  Pallas kernels: 61 us -> 49.1 us
    pallas_call x1, Pallas kernels: 61 us -> 49.1 us  [per_device(): pl.pallas_call(functools.partial(kernel, tiles), out_shape=jax.ShapeDtype...]
where the time goes in v2:
time: 51.4 us; the launch traced here: 50.9 us
  Pallas kernels  49.1 us (96%)
  local copies, waits for them, and re-layouts  1.75 us (3%)
    pallas_call x1, Pallas kernels, per_device(): pl.pallas_call(functools.partial(kernel, tiles), out_shape=jax.ShapeDtype...  49.1 us
    unnamed x1, local copies, waits for them, and re-layouts  1.75 us

profile of v2, /device:TPU:1, one launch (start us, length us, event | category | flops | bytes accessed | tf_op | source)
XLA Modules:
  0.0 50.9 jit_solution(13987605343968208780)
XLA Ops:
  0.0 49.1 %shard_map.100 = f32[2,90,4,128]{3,2,1,0:T(4,128)} custom-call(bf16[2,90,4,128]{3,2,1,0:T(4,128)(2,1)} %fwd.1, bf16[90,4,128]{2,1,0:T(4,128)(2,1)} %kap.1, s32[1,1,128]{2,1,0:T(1,128)} %send_order.1, s32[1,1,128]{2,1,0:T(1,128)} %recv_place.1, s32[4,128]{1,0:T(4,128)} %depth.1, f32[90]{0:T(128)} %rate_in.1, f32[2,90,4,128]{3,2,1,0:T(4,128)} %adj.1, ...), custom_call_target="tpu_custom_call" | custom-call | flops 1000000000 | bytes 4194304 | tf_op jit(solution)/shard_map/pallas_call | solution.py:486
  49.1 1.7 %copy.12 = f32[2,90,4,128]{3,2,1,0:T(4,128)} copy(f32[2,90,4,128]{3,2,1,0:T(4,128)} %shard_map.100) | data formatting | bytes 737280

commit v3 on v2

--- a/solution.py
+++ b/solution.py
@@ -52,7 +52,7 @@
     coup_v, stage, send_one, land_one,
     meta, metas, half_adj, half_mis, edge_adj, halo_adj, halo_mis, halo_edge, own_adj, own_mis,
     placed, state, middle, keep, factor, inverse, source,
-    final, other, send_two, land_two, stage_pair, stage_two,
+    final, other, send_two, land_two, stage_pair,
     local, meta_sem, one_sem, pass_sem, halo_sem, pair_sem, two_sem,
 ):
     tile = lax.axis_index("tile")
@@ -97,7 +97,7 @@
     fwd_v[1, LEV] = jnp.zeros((4, LANES), BF16)
     kap_v[LEV] = jnp.zeros((4, LANES), BF16)
     coup_v[pl.ds(4 * LEV, 24)] = jnp.zeros((24, LANES), F32)
-    stage[:, 3, :] = jnp.zeros((LANES, LANES), F32)
+    stage[:, 4, 1, :] = jnp.zeros((LANES, LANES), F32)
 
     for move in moves[:4]:
         move.wait()
@@ -125,12 +125,12 @@
 
     pick = in_slot(so_v[...]).T.astype(BF16)
     pieces = column_dot(pick, coup_v[...].astype(BF16))
-    for part in range(3):
-        stage[:, part, :] = pieces[:, part * LANES : (part + 1) * LANES]
-    packed = stage[...].astype(BF16)
-    send_one[pl.ds(1, tiles)] = packed
-    send_one[0] = packed[tiles - 1]
-    send_one[tiles + 1] = packed[0]
+    for beside in range(3):
+        moved = pieces if beside == 1 else pltpu.roll(pieces, (1 - beside) % tiles, 0)
+        for part in range(3):
+            at = 3 * beside + part
+            stage[:, at // 2, at % 2, :] = moved[:, part * LANES : (part + 1) * LANES]
+    send_one[...] = stage[...].astype(BF16)
 
     moves[4].wait()
     meta[0] = jnp.concatenate([depth_v[...], depth_v[...]], axis=0)
@@ -139,8 +139,19 @@
     moves[5].wait()
     for tracer in range(2):
         half_adj[tracer] = adj_v[tracer].astype(BF16)
-        edge_adj[0, tracer] = adj_v[tracer, :, 3:4, :]
-        edge_adj[1, tracer] = adj_v[tracer, :, 0:1, :]
+
+    def outline(block, carry):
+        for pair in range(3):
+            level = 2 * (block * 3 + pair)
+            for tracer in range(2):
+                for side, line in ((0, 3), (1, 0)):
+                    rows = [adj_v[tracer, level + half, line : line + 1, :] for half in range(2)]
+                    edge_adj[side, tracer, block * 3 + pair] = jnp.concatenate(
+                        rows, axis=0
+                    ).astype(BF16)
+        return carry
+
+    lax.fori_loop(0, LEV // 6, outline, 0)
     moves[6].wait()
     for tracer in range(2):
         half_mis[tracer] = mis_v[tracer].astype(BF16)
@@ -170,13 +181,13 @@
     def route_one(step, carry):
         to = lax.rem(tile + step, tiles)
         remote(
-            send_one.at[pl.ds(to, 3)], land_one.at[0, tile], one_sem.at[0], one_sem.at[1], face, to
+            send_one.at[to], land_one.at[0, tile], one_sem.at[0], one_sem.at[1], face, to
         )
         return carry
 
     lax.fori_loop(1, tiles, route_one, 0)
     self_one = pltpu.make_async_copy(
-        send_one.at[pl.ds(tile, 3)], land_one.at[0, tile], local.at[12]
+        send_one.at[tile], land_one.at[0, tile], local.at[12]
     )
     self_one.start()
     for side, shift in SIDES:
@@ -257,25 +268,31 @@
             arrived(halo_edge, halo_sem.at[3])
 
             def begin(block, carry):
-                for inner in range(5):
-                    level = block * 5 + inner
+                for inner in range(6):
+                    level = block * 6 + inner
+                    lines = [
+                        halo_edge[i, block * 3 + inner // 2].astype(F32)[inner % 2 : inner % 2 + 1]
+                        for i in range(4)
+                    ]
                     tile_of = {
                         1: stack_faces(1, halo_adj[0, level].astype(F32), halo_adj[1, level].astype(F32)),
                         2: stack_faces(2, own_adj[0, level], own_adj[1, level]),
                         3: stack_faces(3, halo_adj[2, level].astype(F32), halo_adj[3, level].astype(F32)),
-                        0: jnp.where(low_row, halo_edge[0, level], halo_edge[1, level]),
-                        4: jnp.where(low_row, halo_edge[2, level], halo_edge[3, level]),
+                        0: jnp.where(low_row, lines[0], lines[1]),
+                        4: jnp.where(low_row, lines[2], lines[3]),
                     }
                     for slot in range(5):
                         state[level, slot] = jnp.where(wet(level, slot), tile_of[slot], 0.0)
                 return carry
 
-            lax.fori_loop(0, LEV // 5, begin, 0)
+            lax.fori_loop(0, LEV // 6, begin, 0)
             arrived(land_one.at[1], pass_sem.at[1])
         which = face if source_of == 0 else 1 - face
+        stage[...] = land_one[source_of].astype(F32)
         for part in range(3):
-            stage[...] = land_one[source_of, :, part].astype(F32)
-            held = jnp.concatenate([stage[:, i, :] for i in range(3)], axis=1).astype(BF16)
+            held = jnp.concatenate(
+                [stage[:, at // 2, at % 2, :] for at in range(3 * part, 3 * part + 3)], axis=1
+            ).astype(BF16)
             place = in_slot(metas[2 * (part + 1) + which, 1][0:1, :]).astype(BF16)
             placed[which, part] = row_dot(held, place)
 
@@ -397,10 +414,10 @@
     end_lane = lax.broadcasted_iota(I32, (LANES, LANES), 1) == LANES - 1
     for source_of in range(2):
         if source_of == 0:
-            values, tracer = final[face], face
+            values = final[face]
         else:
             arrived(other, pair_sem.at[5])
-            values, tracer = other[...], 1 - face
+            values = other[...]
         high = values.astype(BF16)
         low = (values - high.astype(F32)).astype(BF16)
         pieces = column_dot(choose, high) + column_dot(choose, low)
@@ -411,9 +428,7 @@
             column = codes[:, part * LANES : (part + 1) * LANES]
             if part == 2:
                 column = jnp.where(end_lane, octave, column)
-            stage_two[tracer, :, part, :] = column
-    for part in range(6):
-        stage_pair[:, part // 2, part % 2, :] = stage_two[part // 3, :, part % 3, :]
+            stage_pair[:, (3 * source_of + part) // 2, (3 * source_of + part) % 2, :] = column
     send_two[...] = stage_pair[...].astype(I32).astype(I16)
 
     def route_two(step, carry):
@@ -428,9 +443,10 @@
     self_two.wait()
     arrived(land_two.at[pl.ds(0, tiles - 1)], two_sem.at[1])
     stage_pair[...] = land_two[...].astype(I32).astype(F32)
-    for tracer in range(2):
+    for source_of in range(2):
+        tracer = face if source_of == 0 else 1 - face
         values = jnp.concatenate(
-            [stage_pair[:, part // 2, part % 2, :] for part in range(3 * tracer, 3 * tracer + 3)],
+            [stage_pair[:, part // 2, part % 2, :] for part in range(3 * source_of, 3 * source_of + 3)],
             axis=1,
         )
         octave = values[:, 3 * LANES - 1 :]
@@ -468,11 +484,11 @@
         vmem((1, LANES), I32), vmem((1, LANES), I32), vmem((4, LANES), I32),
         vmem((2,) + block, F32), vmem((2,) + block, F32),
         vmem((1, LANES), I32), vmem((1, LANES), I32),
-        vmem((384, LANES), F32), vmem((tiles, 4, LANES), F32),
-        vmem((tiles + 2, 4, LANES), BF16), vmem((2, tiles, 3, 4, LANES), BF16),
+        vmem((384, LANES), F32), vmem((tiles, 5, 2, LANES), F32),
+        vmem((tiles, 5, 2, LANES), BF16), vmem((2, tiles, 5, 2, LANES), BF16),
         vmem((2, 8, LANES), I32), vmem((10, 2, 8, LANES), I32),
-        vmem((2,) + block, BF16), vmem((2,) + block, BF16), vmem((2, 2, LEV, 1, LANES), F32),
-        vmem((4,) + block, BF16), vmem((4,) + block, BF16), vmem((4, LEV, 1, LANES), F32),
+        vmem((2,) + block, BF16), vmem((2,) + block, BF16), vmem((2, 2, LEV // 2, 2, LANES), BF16),
+        vmem((4,) + block, BF16), vmem((4,) + block, BF16), vmem((4, LEV // 2, 2, LANES), BF16),
         vmem((2,) + block, F32), vmem((2,) + block, F32),
         vmem((2, 3, 384, LANES), F32), vmem((LEV, 5, 8, LANES), F32),
         vmem(level_rows, F32), vmem(level_rows, F32), vmem(level_rows, F32),
@@ -480,7 +496,6 @@
         vmem((2, 384, LANES), F32), vmem((384, LANES), F32),
         vmem((tiles, 3, 2, LANES), I16), vmem((tiles, 3, 2, LANES), I16),
         vmem((tiles, 3, 2, LANES), F32),
-        vmem((2, tiles, 3, LANES), F32),
         dma((14,)), dma((2,)), dma((2,)), dma((2,)), dma((6,)), dma((6,)), dma((2,)),
     ]
     return pl.pallas_call(

time: 51.4 us -> 48.3 us (0.940)
  Pallas kernels: 49.1 us -> 45.9 us
    pallas_call x1, Pallas kernels: 49.1 us -> 45.9 us  [per_device(): pl.pallas_call(functools.partial(kernel, tiles), out_shape=jax.ShapeDtype...]
where the time goes in v3:
time: 48.3 us; the launch traced here: 47.7 us
  Pallas kernels  45.9 us (95%)
  local copies, waits for them, and re-layouts  1.75 us (4%)
    pallas_call x1, Pallas kernels, per_device(): pl.pallas_call(functools.partial(kernel, tiles), out_shape=jax.ShapeDtype...  45.9 us
    unnamed x1, local copies, waits for them, and re-layouts  1.75 us

profile of v3, /device:TPU:1, one launch (start us, length us, event | category | flops | bytes accessed | tf_op | source)
XLA Modules:
  0.0 47.7 jit_solution(7218878942315577985)
XLA Ops:
  0.0 45.9 %shard_map.100 = f32[2,90,4,128]{3,2,1,0:T(4,128)} custom-call(bf16[2,90,4,128]{3,2,1,0:T(4,128)(2,1)} %fwd.1, bf16[90,4,128]{2,1,0:T(4,128)(2,1)} %kap.1, s32[1,1,128]{2,1,0:T(1,128)} %send_order.1, s32[1,1,128]{2,1,0:T(1,128)} %recv_place.1, s32[4,128]{1,0:T(4,128)} %depth.1, f32[90]{0:T(128)} %rate_in.1, f32[2,90,4,128]{3,2,1,0:T(4,128)} %adj.1, ...), custom_call_target="tpu_custom_call" | custom-call | flops 1000000000 | bytes 4194304 | tf_op jit(solution)/shard_map/pallas_call | solution.py:501
  45.9 1.7 %copy.12 = f32[2,90,4,128]{3,2,1,0:T(4,128)} copy(f32[2,90,4,128]{3,2,1,0:T(4,128)} %shard_map.100) | data formatting | bytes 737280

commit v4 on v3

--- a/solution.py
+++ b/solution.py
@@ -47,12 +47,12 @@
 def kernel(
     tiles,
     fwd, kap, send_order, recv_place, depth, rate_in, adj, mis, ctrl_send, ctrl_place,
-    out,
+    land_two,
     rate, fwd_v, kap_v, so_v, rp_v, depth_v, adj_v, mis_v, cs_v, cp_v,
     coup_v, stage, send_one, land_one,
     meta, metas, half_adj, half_mis, edge_adj, halo_adj, halo_mis, halo_edge, own_adj, own_mis,
-    placed, state, middle, keep, factor, inverse, source,
-    final, other, send_two, land_two, stage_pair,
+    placed, give, take, state, middle, keep, factor, inverse, source,
+    final, other, send_two, stage_pair,
     local, meta_sem, one_sem, pass_sem, halo_sem, pair_sem, two_sem,
 ):
     tile = lax.axis_index("tile")
@@ -181,13 +181,13 @@
     def route_one(step, carry):
         to = lax.rem(tile + step, tiles)
         remote(
-            send_one.at[to], land_one.at[0, tile], one_sem.at[0], one_sem.at[1], face, to
+            send_one.at[to], land_one.at[tile], one_sem.at[0], one_sem.at[1], face, to
         )
         return carry
 
     lax.fori_loop(1, tiles, route_one, 0)
     self_one = pltpu.make_async_copy(
-        send_one.at[tile], land_one.at[0, tile], local.at[12]
+        send_one.at[tile], land_one.at[tile], local.at[12]
     )
     self_one.start()
     for side, shift in SIDES:
@@ -258,43 +258,46 @@
     lax.fori_loop(0, LEV // 5, prepare, 0)
 
     self_one.wait()
-    arrived(land_one.at[0, pl.ds(0, tiles - 1)], one_sem.at[1])
-    remote(land_one.at[0], land_one.at[1], pass_sem.at[0], pass_sem.at[1], 1 - face, tile)
-    for source_of in range(2):
-        if source_of == 1:
-            moves[9].wait()
-            arrived(own_adj.at[0], pair_sem.at[1])
-            arrived(halo_adj, halo_sem.at[1])
-            arrived(halo_edge, halo_sem.at[3])
-
-            def begin(block, carry):
-                for inner in range(6):
-                    level = block * 6 + inner
-                    lines = [
-                        halo_edge[i, block * 3 + inner // 2].astype(F32)[inner % 2 : inner % 2 + 1]
-                        for i in range(4)
-                    ]
-                    tile_of = {
-                        1: stack_faces(1, halo_adj[0, level].astype(F32), halo_adj[1, level].astype(F32)),
-                        2: stack_faces(2, own_adj[0, level], own_adj[1, level]),
-                        3: stack_faces(3, halo_adj[2, level].astype(F32), halo_adj[3, level].astype(F32)),
-                        0: jnp.where(low_row, lines[0], lines[1]),
-                        4: jnp.where(low_row, lines[2], lines[3]),
-                    }
-                    for slot in range(5):
-                        state[level, slot] = jnp.where(wet(level, slot), tile_of[slot], 0.0)
-                return carry
-
-            lax.fori_loop(0, LEV // 6, begin, 0)
-            arrived(land_one.at[1], pass_sem.at[1])
-        which = face if source_of == 0 else 1 - face
-        stage[...] = land_one[source_of].astype(F32)
-        for part in range(3):
-            held = jnp.concatenate(
-                [stage[:, at // 2, at % 2, :] for at in range(3 * part, 3 * part + 3)], axis=1
-            ).astype(BF16)
-            place = in_slot(metas[2 * (part + 1) + which, 1][0:1, :]).astype(BF16)
-            placed[which, part] = row_dot(held, place)
+    arrived(land_one.at[pl.ds(0, tiles - 1)], one_sem.at[1])
+    stage[...] = land_one[...].astype(F32)
+    for part in range(3):
+        held = jnp.concatenate(
+            [stage[:, at // 2, at % 2, :] for at in range(3 * part, 3 * part + 3)], axis=1
+        ).astype(BF16)
+        place = in_slot(metas[2 * (part + 1) + face, 1][0:1, :]).astype(BF16)
+        result = row_dot(held, place)
+        give[part] = result.astype(BF16)
+        remote(
+            give.at[part], take.at[part], pass_sem.at[part], pass_sem.at[3 + part], 1 - face, tile
+        )
+        placed[face, part] = result
+    moves[9].wait()
+    arrived(own_adj.at[0], pair_sem.at[1])
+    arrived(halo_adj, halo_sem.at[1])
+    arrived(halo_edge, halo_sem.at[3])
+
+    def begin(block, carry):
+        for inner in range(6):
+            level = block * 6 + inner
+            lines = [
+                halo_edge[i, block * 3 + inner // 2].astype(F32)[inner % 2 : inner % 2 + 1]
+                for i in range(4)
+            ]
+            tile_of = {
+                1: stack_faces(1, halo_adj[0, level].astype(F32), halo_adj[1, level].astype(F32)),
+                2: stack_faces(2, own_adj[0, level], own_adj[1, level]),
+                3: stack_faces(3, halo_adj[2, level].astype(F32), halo_adj[3, level].astype(F32)),
+                0: jnp.where(low_row, lines[0], lines[1]),
+                4: jnp.where(low_row, lines[2], lines[3]),
+            }
+            for slot in range(5):
+                state[level, slot] = jnp.where(wet(level, slot), tile_of[slot], 0.0)
+        return carry
+
+    lax.fori_loop(0, LEV // 6, begin, 0)
+    for part in range(3):
+        arrived(take.at[part], pass_sem.at[3 + part])
+        placed[1 - face, part] = take[part].astype(F32)
 
     one = jnp.ones((8, LANES), F32)
 
@@ -439,9 +442,25 @@
     lax.fori_loop(1, tiles, route_two, 0)
     self_two = pltpu.make_async_copy(send_two.at[tile], land_two.at[tile], local.at[13])
     self_two.start()
-    place = in_slot(cp_v[...]).astype(BF16)
     self_two.wait()
     arrived(land_two.at[pl.ds(0, tiles - 1)], two_sem.at[1])
+
+    arrived(metas.at[pl.ds(0, 9)], meta_sem.at[0])
+    arrived(own_adj.at[0], pair_sem.at[0])
+    arrived(own_mis.at[0], pair_sem.at[2])
+    arrived(land_one.at[pl.ds(0, tiles - 1)], one_sem.at[0])
+    arrived(halo_adj, halo_sem.at[0])
+    arrived(halo_edge, halo_sem.at[2])
+    arrived(halo_mis, halo_sem.at[4])
+    for part in range(3):
+        arrived(give.at[part], pass_sem.at[part])
+    arrived(other, pair_sem.at[4])
+    arrived(land_two.at[pl.ds(0, tiles - 1)], two_sem.at[0])
+
+
+def deliver(land_two, cp_v, out, stage_pair):
+    face = lax.axis_index("face")
+    place = in_slot(cp_v[0]).astype(BF16)
     stage_pair[...] = land_two[...].astype(I32).astype(F32)
     for source_of in range(2):
         tracer = face if source_of == 0 else 1 - face
@@ -455,17 +474,6 @@
         low = (values - high.astype(F32)).astype(BF16)
         result = row_dot(high, place) + row_dot(low, place)
         out[tracer] = result[: 4 * LEV].reshape(LEV, 4, LANES)
-
-    arrived(metas.at[pl.ds(0, 9)], meta_sem.at[0])
-    arrived(own_adj.at[0], pair_sem.at[0])
-    arrived(own_mis.at[0], pair_sem.at[2])
-    arrived(land_one.at[0, pl.ds(0, tiles - 1)], one_sem.at[0])
-    arrived(halo_adj, halo_sem.at[0])
-    arrived(halo_edge, halo_sem.at[2])
-    arrived(halo_mis, halo_sem.at[4])
-    arrived(land_one.at[1], pass_sem.at[0])
-    arrived(other, pair_sem.at[4])
-    arrived(land_two.at[pl.ds(0, tiles - 1)], two_sem.at[0])
 
 
 def per_device(
@@ -485,24 +493,25 @@
         vmem((2,) + block, F32), vmem((2,) + block, F32),
         vmem((1, LANES), I32), vmem((1, LANES), I32),
         vmem((384, LANES), F32), vmem((tiles, 5, 2, LANES), F32),
-        vmem((tiles, 5, 2, LANES), BF16), vmem((2, tiles, 5, 2, LANES), BF16),
+        vmem((tiles, 5, 2, LANES), BF16), vmem((tiles, 5, 2, LANES), BF16),
         vmem((2, 8, LANES), I32), vmem((10, 2, 8, LANES), I32),
         vmem((2,) + block, BF16), vmem((2,) + block, BF16), vmem((2, 2, LEV // 2, 2, LANES), BF16),
         vmem((4,) + block, BF16), vmem((4,) + block, BF16), vmem((4, LEV // 2, 2, LANES), BF16),
         vmem((2,) + block, F32), vmem((2,) + block, F32),
-        vmem((2, 3, 384, LANES), F32), vmem((LEV, 5, 8, LANES), F32),
+        vmem((2, 3, 384, LANES), F32), vmem((3, 384, LANES), BF16), vmem((3, 384, LANES), BF16),
+        vmem((LEV, 5, 8, LANES), F32),
         vmem(level_rows, F32), vmem(level_rows, F32), vmem(level_rows, F32),
         vmem(level_rows, F32), vmem(level_rows, F32),
         vmem((2, 384, LANES), F32), vmem((384, LANES), F32),
-        vmem((tiles, 3, 2, LANES), I16), vmem((tiles, 3, 2, LANES), I16),
+        vmem((tiles, 3, 2, LANES), I16),
         vmem((tiles, 3, 2, LANES), F32),
-        dma((14,)), dma((2,)), dma((2,)), dma((2,)), dma((6,)), dma((6,)), dma((2,)),
+        dma((14,)), dma((2,)), dma((2,)), dma((6,)), dma((6,)), dma((6,)), dma((2,)),
     ]
-    return pl.pallas_call(
+    landed = pl.pallas_call(
         functools.partial(kernel, tiles),
-        out_shape=jax.ShapeDtypeStruct((2,) + block, F32),
+        out_shape=jax.ShapeDtypeStruct((tiles, 3, 2, LANES), I16),
         in_specs=[anywhere] * 10,
-        out_specs=pl.BlockSpec(memory_space=pltpu.VMEM),
+        out_specs=pl.BlockSpec(memory_space=pl.ANY),
         scratch_shapes=scratch,
         compiler_params=pltpu.CompilerParams(
             collective_id=0, has_side_effects=True, vmem_limit_bytes=60 * 2**20
@@ -514,6 +523,14 @@
         fwd_tracers, fwd_kappa, send_order, recv_place, depth_levels, horiz_rate, adj_init, misfit,
         ctrl_send, ctrl_place,
     )
+    return pl.pallas_call(
+        deliver,
+        out_shape=jax.ShapeDtypeStruct((2,) + block, F32),
+        in_specs=[pl.BlockSpec(memory_space=pltpu.VMEM)] * 2,
+        out_specs=pl.BlockSpec(memory_space=pltpu.VMEM),
+        scratch_shapes=[vmem((tiles, 3, 2, LANES), F32)],
+        compiler_params=pltpu.CompilerParams(vmem_limit_bytes=60 * 2**20),
+    )(landed, ctrl_place)
 
 
 def solution(mesh):

time: 48.3 us -> 47.6 us (0.986)
  local copies, waits for them, and re-layouts: 1.75 us -> 0 us
  Pallas kernels: 45.9 us -> 47.1 us
    pallas_call x0 -> x1, Pallas kernels: none -> 2.38 us  [per_device(): pl.pallas_call(deliver, out_shape=jax.ShapeDtypeStruct((2,) + block, F32)...]
    unnamed x1 -> x0, local copies, waits for them, and re-layouts: 1.75 us -> none
    pallas_call x1, Pallas kernels: 45.9 us -> 44.7 us  [per_device(): pl.pallas_call(functools.partial(kernel, tiles), out_shape=jax.ShapeDtype...]
where the time goes in v4:
time: 47.6 us; the launch traced here: 47.1 us
  Pallas kernels  47.1 us (99%)
    pallas_call x1, Pallas kernels, per_device(): pl.pallas_call(functools.partial(kernel, tiles), out_shape=jax.ShapeDtype...  44.7 us
    pallas_call x1, Pallas kernels, per_device(): pl.pallas_call(deliver, out_shape=jax.ShapeDtypeStruct((2,) + block, F32)...  2.38 us

profile of v4, /device:TPU:1, one launch (start us, length us, event | category | flops | bytes accessed | tf_op | source)
XLA Modules:
  0.0 47.1 jit_solution(1941636107014434753)
XLA Ops:
  0.0 44.7 %shard_map.100.land_two = s16[128,3,2,128]{3,2,1,0:T(2,128)(2,1)} custom-call(bf16[2,90,4,128]{3,2,1,0:T(4,128)(2,1)} %fwd.1, bf16[90,4,128]{2,1,0:T(4,128)(2,1)} %kap.1, s32[1,1,128]{2,1,0:T(1,128)} %send_order.1, s32[1,1,128]{2,1,0:T(1,128)} %recv_place.1, s32[4,128]{1,0:T(4,128)} %depth.1, f32[90]{0:T(128)} %rate_in.1, f32[2,90,4,128]{3,2,1,0:T(4,128)} %adj.1, ...), custom_call_target="tpu_custom_call" | custom-call | flops 1000000000 | bytes 4194304 | tf_op jit(solution)/shard_map/pallas_call | solution.py:510
  44.7 2.4 %shard_map.101 = f32[2,90,4,128]{3,2,1,0:T(4,128)} custom-call(s16[128,3,2,128]{3,2,1,0:T(2,128)(2,1)} %shard_map.100.land_two, s32[1,1,128]{2,1,0:T(1,128)} %cp_v.1), custom_call_target="tpu_custom_call" | custom-call | tf_op jit(solution)/shard_map/pallas_call | solution.py:526

commit v5 on v4

--- a/solution.py
+++ b/solution.py
@@ -17,7 +17,6 @@
 STEPS = 5
 LANES = 128
 UNROLL = 10
-SWEEP = 90
 CODE = 32000.0
 SIDES = ((0, 1), (1, -1))
 
@@ -51,7 +50,7 @@
     rate, fwd_v, kap_v, so_v, rp_v, depth_v, adj_v, mis_v, cs_v, cp_v,
     coup_v, stage, send_one, land_one,
     meta, metas, half_adj, half_mis, edge_adj, halo_adj, halo_mis, halo_edge, own_adj, own_mis,
-    placed, give, take, state, middle, keep, factor, inverse, source,
+    places, placed, give, take, state, middle, keep, factor, inverse, source,
     final, other, send_two, stage_pair,
     local, meta_sem, one_sem, pass_sem, halo_sem, pair_sem, two_sem,
 ):
@@ -216,14 +215,17 @@
     first_cell, last_cell = cell == 0, cell == 3
     first_lane, last_lane = lane == 0, lane == LANES - 1
     low_lane, low_row = lane < LANES // 2, row < 4
+    east_wing = cell < 2
     seam_even = low_lane == low_row
     seam_odd = low_lane != low_row
 
-    def neighbours(slot, west, here, east):
+    def neighbours(slot, west, here, east, to_west=None, to_east=None):
+        to_west = here if to_west is None else to_west
+        to_east = here if to_east is None else to_east
         seam = jnp.where(seam_even if slot % 2 == 0 else seam_odd, pltpu.roll(here, 4, 0), 0.0)
         return (
-            pltpu.roll(jnp.where(first_cell, east, here), 7, 0),
-            pltpu.roll(jnp.where(last_cell, west, here), 1, 0),
+            pltpu.roll(jnp.where(first_cell, east, to_east), 7, 0),
+            pltpu.roll(jnp.where(last_cell, west, to_west), 1, 0),
             pltpu.roll(jnp.where(first_lane, seam, here), LANES - 1, 1),
             pltpu.roll(jnp.where(last_lane, seam, here), 1, 1),
         )
@@ -242,18 +244,27 @@
     def wet(level, slot):
         return level.astype(F32) < depths[slot]
 
+    def store_wing(ref, level, values):
+        for i in range(3):
+            ref[level, i] = values[i]
+        ref[level, 3] = jnp.where(east_wing, values[2], values[0])
+
     def prepare(block, carry):
         for inner in range(5):
             level = block * 5 + inner
             at = level.astype(F32)
             speed = rate[level]
+            kept = []
             for slot in (1, 2, 3):
                 count = jnp.zeros((8, LANES), F32)
                 for beside in around[slot - 1]:
                     count = count + jnp.where(at < beside, 1.0, 0.0)
-                keep[level, slot - 1] = 1.0 - speed * count
-        return carry
-
+                kept.append(1.0 - speed * count)
+            store_wing(keep, level, kept)
+        return carry
+
+    for part in range(3):
+        places[part] = in_slot(metas[2 * (part + 1) + face, 1][0:1, :]).astype(BF16)
     moves[11].wait()
     lax.fori_loop(0, LEV // 5, prepare, 0)
 
@@ -264,8 +275,7 @@
         held = jnp.concatenate(
             [stage[:, at // 2, at % 2, :] for at in range(3 * part, 3 * part + 3)], axis=1
         ).astype(BF16)
-        place = in_slot(metas[2 * (part + 1) + face, 1][0:1, :]).astype(BF16)
-        result = row_dot(held, place)
+        result = row_dot(held, places[part])
         give[part] = result.astype(BF16)
         remote(
             give.at[part], take.at[part], pass_sem.at[part], pass_sem.at[3 + part], 1 - face, tile
@@ -305,6 +315,7 @@
         carry = [(upper / lower, one) for upper, lower in carry]
         for pair in range(UNROLL // 2):
             base = pl.multiple_of(block * (4 * UNROLL) + pair * 8, 8)
+            factors, inverses = ([], []), ([], [])
             for slot in (1, 2, 3):
                 first, second = ordered(
                     slot, placed[0, slot - 1, pl.ds(base, 8)], placed[1, slot - 1, pl.ds(base, 8)]
@@ -322,69 +333,74 @@
                     next_lower = upper + weight * lower
                     next_upper = next_lower + weight * upper
                     ratio = lower / next_lower
-                    factor[level, slot - 1] = weight * ratio
-                    inverse[level, slot - 1] = jnp.where(wet(level, slot), ratio, 0.0)
+                    factors[half].append(weight * ratio)
+                    inverses[half].append(jnp.where(wet(level, slot), ratio, 0.0))
                     upper, lower = next_upper, next_lower
                 carry[slot - 1] = (upper, lower)
+            for half in range(2):
+                level = block * UNROLL + pair * 2 + half
+                store_wing(factor, level, factors[half])
+                store_wing(inverse, level, inverses[half])
         return carry
 
     lax.fori_loop(0, LEV // UNROLL, eliminate, [(one, one)] * 3)
 
     zero = jnp.zeros((8, LANES), F32)
 
-    def descend(slots, block, carry):
-        carry = list(carry)
-        for inner in range(SWEEP):
-            level = block * SWEEP + inner
+    def across(slots, folding, level):
+        held = {
+            slot: state[level, slot]
+            for slot in ((0, 1, 2, 3, 4) if 1 in slots else (1, 2, 3) if folding else (2, 5))
+        }
+        if 1 in slots:
+            return [(held[slot], neighbours(slot, held[slot - 1], held[slot], held[slot + 1])) for slot in slots]
+        here = held[2]
+        if folding:
+            west, east = held[1], held[3]
+            wing = jnp.where(east_wing, east, west)
+            to_east = jnp.where(last_cell, west, east)
+            to_west = jnp.where(first_cell, east, west)
+        else:
+            west = east = wing = to_east = to_west = held[5]
+        found = [(here, neighbours(2, west, here, east))]
+        if 5 in slots:
+            found.append((wing, neighbours(5, here, wing, here, to_west, to_east)))
+        return found
+
+    def descend(slots, folding=False):
+        carry = [zero] * len(slots)
+        for level in range(LEV):
             speed = rate[level]
-            tile_of = {
-                slot: state[level, slot] for slot in range(slots[0] - 1, slots[-1] + 2)
-            }
-            for i, slot in enumerate(slots):
-                east, west, north, south = neighbours(
-                    slot, tile_of[slot - 1], tile_of[slot], tile_of[slot + 1]
+            for i, (here, (east, west, north, south)) in enumerate(across(slots, folding, level)):
+                at = slots[i] - 1 if slots[i] < 5 else 3
+                value = (
+                    keep[level, at] * here + speed * ((east + west) + (north + south)) + carry[i]
                 )
-                spread = keep[level, slot - 1] * tile_of[slot] + speed * (
-                    (east + west) + (north + south)
-                )
-                value = spread + carry[i]
-                middle[level, slot - 1] = value
-                carry[i] = factor[level, slot - 1] * value
-        return carry
-
-    def ascend(slots, last, block, carry):
-        carry = list(carry)
-        for pair in range(SWEEP // 2):
+                middle[level, at] = value
+                carry[i] = factor[level, at] * value
+
+    def ascend(slots, last=False):
+        carry = [zero] * len(slots)
+        for pair in range(LEV // 2):
             halves = []
             for inner in range(2):
-                level = (LEV - 1) - (block * SWEEP + pair * 2 + inner)
+                level = LEV - 1 - (2 * pair + inner)
                 for i, slot in enumerate(slots):
-                    solved = (
-                        middle[level, slot - 1] * inverse[level, slot - 1]
-                        + factor[level, slot - 1] * carry[i]
-                    )
+                    at = slot - 1 if slot < 5 else 3
+                    solved = middle[level, at] * inverse[level, at] + factor[level, at] * carry[i]
                     carry[i] = solved
-                    value = solved + source[level, slot - 1]
+                    value = solved + source[level, at]
                     if last:
                         halves.append(value)
                     else:
                         state[level, slot] = value
             if last:
                 below, above = halves
-                base = pl.multiple_of(
-                    (4 * LEV - 8) - (block * (4 * SWEEP) + pair * 8), 8
-                )
+                base = 4 * LEV - 8 - 8 * pair
                 final[0, pl.ds(base, 8)] = jnp.where(low_row, above, pltpu.roll(below, 4, 0))
                 final[1, pl.ds(base, 8)] = jnp.where(low_row, pltpu.roll(above, 4, 0), below)
-        return carry
-
-    def advance(step, carry):
-        lax.fori_loop(0, LEV // SWEEP, functools.partial(descend, (1, 2, 3)), [zero] * 3)
-        lax.fori_loop(0, LEV // SWEEP, functools.partial(ascend, (1, 2, 3), False), [zero] * 3)
-        return carry
-
-    sweep_down = functools.partial(descend, (1, 2, 3))
-    lax.fori_loop(0, LEV // SWEEP, sweep_down, [zero] * 3)
+
+    descend((1, 2, 3))
     moves[10].wait()
     arrived(own_mis.at[0], pair_sem.at[3])
     arrived(halo_mis, halo_sem.at[5])
@@ -397,18 +413,26 @@
                 2: stack_faces(2, own_mis[0, level], own_mis[1, level]),
                 3: stack_faces(3, halo_mis[2, level].astype(F32), halo_mis[3, level].astype(F32)),
             }
-            for slot in (1, 2, 3):
-                source[level, slot - 1] = jnp.where(wet(level, slot), tile_of[slot], 0.0)
+            store_wing(
+                source, level,
+                [jnp.where(wet(level, slot), tile_of[slot], 0.0) for slot in (1, 2, 3)],
+            )
         return carry
 
     lax.fori_loop(0, LEV // 5, drive, 0)
 
-    lax.fori_loop(0, LEV // SWEEP, functools.partial(ascend, (1, 2, 3), False), [zero] * 3)
-    lax.fori_loop(1, STEPS - 1, advance, 0)
-    lax.fori_loop(0, LEV // SWEEP, functools.partial(descend, (2,)), [zero])
+    ascend((1, 2, 3))
+    descend((1, 2, 3))
+    ascend((1, 2, 3))
+    descend((2, 5), folding=True)
+    ascend((2, 5))
+    for step in range(3, STEPS - 1):
+        descend((2, 5))
+        ascend((2, 5))
     final[0, pl.ds(4 * LEV, 24)] = jnp.zeros((24, LANES), F32)
     final[1, pl.ds(4 * LEV, 24)] = jnp.zeros((24, LANES), F32)
-    lax.fori_loop(0, LEV // SWEEP, functools.partial(ascend, (2,), True), [zero])
+    descend((2,))
+    ascend((2,), last=True)
 
     remote(final.at[1 - face], other, pair_sem.at[4], pair_sem.at[5], 1 - face, tile)
     moves[7].wait()
@@ -485,7 +509,7 @@
     vmem = pltpu.VMEM
     dma = pltpu.SemaphoreType.DMA
     block = (LEV, 4, LANES)
-    level_rows = (LEV, 3, 8, LANES)
+    level_rows = (LEV, 4, 8, LANES)
     scratch = [
         pltpu.SMEM((LEV,), F32),
         vmem((2, LEV + 1, 4, LANES), BF16), vmem((LEV + 1, 4, LANES), BF16),
@@ -498,8 +522,9 @@
         vmem((2,) + block, BF16), vmem((2,) + block, BF16), vmem((2, 2, LEV // 2, 2, LANES), BF16),
         vmem((4,) + block, BF16), vmem((4,) + block, BF16), vmem((4, LEV // 2, 2, LANES), BF16),
         vmem((2,) + block, F32), vmem((2,) + block, F32),
+        vmem((3, LANES, LANES), BF16),
         vmem((2, 3, 384, LANES), F32), vmem((3, 384, LANES), BF16), vmem((3, 384, LANES), BF16),
-        vmem((LEV, 5, 8, LANES), F32),
+        vmem((LEV, 6, 8, LANES), F32),
         vmem(level_rows, F32), vmem(level_rows, F32), vmem(level_rows, F32),
         vmem(level_rows, F32), vmem(level_rows, F32),
         vmem((2, 384, LANES), F32), vmem((384, LANES), F32),

time: 47.6 us -> 47.3 us (level)
  no operation moved by 1% of the time
where the time goes in v5:
time: 47.3 us; the launch traced here: 46.8 us
  Pallas kernels  46.8 us (99%)
    pallas_call x1, Pallas kernels, per_device(): pl.pallas_call(functools.partial(kernel, tiles), out_shape=jax.ShapeDtype...  44.4 us
    pallas_call x1, Pallas kernels, per_device(): pl.pallas_call(deliver, out_shape=jax.ShapeDtypeStruct((2,) + block, F32)...  2.37 us

profile of v5, /device:TPU:1, one launch (start us, length us, event | category | flops | bytes accessed | tf_op | source)
XLA Modules:
  0.0 46.8 jit_solution(22244366014861549)
XLA Ops:
  0.0 44.4 %shard_map.100.land_two = s16[128,3,2,128]{3,2,1,0:T(2,128)(2,1)} custom-call(bf16[2,90,4,128]{3,2,1,0:T(4,128)(2,1)} %fwd.1, bf16[90,4,128]{2,1,0:T(4,128)(2,1)} %kap.1, s32[1,1,128]{2,1,0:T(1,128)} %send_order.1, s32[1,1,128]{2,1,0:T(1,128)} %recv_place.1, s32[4,128]{1,0:T(4,128)} %depth.1, f32[90]{0:T(128)} %rate_in.1, f32[2,90,4,128]{3,2,1,0:T(4,128)} %adj.1, ...), custom_call_target="tpu_custom_call" | custom-call | flops 1000000000 | bytes 4194304 | tf_op jit(solution)/shard_map/pallas_call | solution.py:535
  44.4 2.4 %shard_map.101 = f32[2,90,4,128]{3,2,1,0:T(4,128)} custom-call(s16[128,3,2,128]{3,2,1,0:T(2,128)(2,1)} %shard_map.100.land_two, s32[1,1,128]{2,1,0:T(1,128)} %cp_v.1), custom_call_target="tpu_custom_call" | custom-call | tf_op jit(solution)/shard_map/pallas_call | solution.py:551

commit v6 on v5

--- a/solution.py
+++ b/solution.py
@@ -379,6 +379,12 @@
                 middle[level, at] = value
                 carry[i] = factor[level, at] * value
 
+    def swap(first, count, at):
+        rows = pl.ds(first, count)
+        remote(
+            final.at[1 - face, rows], other.at[rows], pair_sem.at[at], pair_sem.at[at + 1], 1 - face, tile
+        )
+
     def ascend(slots, last=False):
         carry = [zero] * len(slots)
         for pair in range(LEV // 2):
@@ -399,6 +405,8 @@
                 base = 4 * LEV - 8 - 8 * pair
                 final[0, pl.ds(base, 8)] = jnp.where(low_row, above, pltpu.roll(below, 4, 0))
                 final[1, pl.ds(base, 8)] = jnp.where(low_row, pltpu.roll(above, 4, 0), below)
+                if base == 176:
+                    swap(176, 208, 6)
 
     descend((1, 2, 3))
     moves[10].wait()
@@ -434,7 +442,7 @@
     descend((2,))
     ascend((2,), last=True)
 
-    remote(final.at[1 - face], other, pair_sem.at[4], pair_sem.at[5], 1 - face, tile)
+    swap(0, 176, 4)
     moves[7].wait()
     moves[8].wait()
     choose = in_slot(cs_v[...]).T.astype(BF16)
@@ -443,7 +451,8 @@
         if source_of == 0:
             values = final[face]
         else:
-            arrived(other, pair_sem.at[5])
+            arrived(other.at[pl.ds(0, 176)], pair_sem.at[5])
+            arrived(other.at[pl.ds(176, 208)], pair_sem.at[7])
             values = other[...]
         high = values.astype(BF16)
         low = (values - high.astype(F32)).astype(BF16)
@@ -478,7 +487,8 @@
     arrived(halo_mis, halo_sem.at[4])
     for part in range(3):
         arrived(give.at[part], pass_sem.at[part])
-    arrived(other, pair_sem.at[4])
+    arrived(other.at[pl.ds(0, 176)], pair_sem.at[4])
+    arrived(other.at[pl.ds(176, 208)], pair_sem.at[6])
     arrived(land_two.at[pl.ds(0, tiles - 1)], two_sem.at[0])
 
 
@@ -530,7 +540,7 @@
         vmem((2, 384, LANES), F32), vmem((384, LANES), F32),
         vmem((tiles, 3, 2, LANES), I16),
         vmem((tiles, 3, 2, LANES), F32),
-        dma((14,)), dma((2,)), dma((2,)), dma((6,)), dma((6,)), dma((6,)), dma((2,)),
+        dma((14,)), dma((2,)), dma((2,)), dma((6,)), dma((6,)), dma((8,)), dma((2,)),
     ]
     landed = pl.pallas_call(
         functools.partial(kernel, tiles),

time: 47.3 us -> 47.2 us (level)
  no operation moved by 1% of the time
where the time goes in v6:
time: 47.2 us; the launch traced here: 46.8 us
  Pallas kernels  46.8 us (99%)
    pallas_call x1, Pallas kernels, per_device(): pl.pallas_call(functools.partial(kernel, tiles), out_shape=jax.ShapeDtype...  44.4 us
    pallas_call x1, Pallas kernels, per_device(): pl.pallas_call(deliver, out_shape=jax.ShapeDtypeStruct((2,) + block, F32)...  2.37 us

profile of v6, /device:TPU:1, one launch (start us, length us, event | category | flops | bytes accessed | tf_op | source)
XLA Modules:
  0.0 46.8 jit_solution(14703633677284311172)
XLA Ops:
  0.0 44.4 %shard_map.100.land_two = s16[128,3,2,128]{3,2,1,0:T(2,128)(2,1)} custom-call(bf16[2,90,4,128]{3,2,1,0:T(4,128)(2,1)} %fwd.1, bf16[90,4,128]{2,1,0:T(4,128)(2,1)} %kap.1, s32[1,1,128]{2,1,0:T(1,128)} %send_order.1, s32[1,1,128]{2,1,0:T(1,128)} %recv_place.1, s32[4,128]{1,0:T(4,128)} %depth.1, f32[90]{0:T(128)} %rate_in.1, f32[2,90,4,128]{3,2,1,0:T(4,128)} %adj.1, ...), custom_call_target="tpu_custom_call" | custom-call | flops 1000000000 | bytes 4194304 | tf_op jit(solution)/shard_map/pallas_call | solution.py:545
  44.4 2.4 %shard_map.101 = f32[2,90,4,128]{3,2,1,0:T(4,128)} custom-call(s16[128,3,2,128]{3,2,1,0:T(2,128)(2,1)} %shard_map.100.land_two, s32[1,1,128]{2,1,0:T(1,128)} %cp_v.1), custom_call_target="tpu_custom_call" | custom-call | tf_op jit(solution)/shard_map/pallas_call | solution.py:561
